TPU v7x, 32 devices: a whole 2x2x4 slice. The times are simulated.
32 devices in a mesh: dp: 8 (over z, core), seq: 4 (over y, x).
Axes of the slice: x: 2, y: 2, z: 4, core: 2. Of those that a mesh axis runs over, the one named last changes fastest.
Arguments:
- query_rows: bfloat16 [8, 512, 2048], P('dp', 'seq'), may hold values from -16 to 16
- key_rows: bfloat16 [8, 512, 2048], P('dp', 'seq'), may hold values from -16 to 16
- value_rows: bfloat16 [8, 512, 2048], P('dp', 'seq'), may hold values from -6 to 6
- out_cotangent: bfloat16 [8, 512, 2048], P('dp', 'seq'), may hold values from -6 to 6
- segment_ids: int32 [8, 512], P('dp'), may hold values from 0 to 7, never falling along the last dimension, each value on 1 to 384 neighbouring positions
- gain_query: float32 [16, 128], P('seq'), may hold values from 0.5 to 6
- gain_key: float32 [16, 128], P('seq'), may hold values from 0.5 to 6
Outputs:
- attended: bfloat16 [8, 512, 2048], P('dp', 'seq')
- grad_query: bfloat16 [8, 512, 2048], P('dp', 'seq')
- grad_key: bfloat16 [8, 512, 2048], P('dp', 'seq')
- grad_value: bfloat16 [8, 512, 2048], P('dp', 'seq')
- grad_gain_query: float32 [16, 128], P('seq')
- grad_gain_key: float32 [16, 128], P('seq')
Inputs may be any that keep to these rules, and one draw needn't show every extreme that they name: `segment_ids`: image number of each token, never falling along the pack; each image with its prompt has 1 to 384 tokens, one exactly 384.
All inputs are finite; a program needn't handle non-finite values.
Results may differ from a plain program's by a relative error of at most 0.0065.
The roundings to bfloat16 on the way count: a program that leaves them out, or rounds other values in their place, can miss the bound.
Values may be sent and summed in bfloat16 or wider, within the bound.
No kernel may reach another device: no remote copies, remote signals or barrier semaphores. Data moves between devices by JAX's collectives and lax.ppermute only.
A program may use at most 64 MiB of HBM per device.

v0:
```python
import functools
import math

import jax
import jax.numpy as jnp
from jax import lax
from jax.experimental import pallas as pl
from jax.experimental.pallas import tpu as pltpu
from jax.sharding import PartitionSpec as P

NEGATIVE = -1e30
EPSILON = 1e-06
VMEM_LIMIT = 48 * 1024 * 1024
ANY = pl.BlockSpec(memory_space=pl.ANY)
HBM = pl.BlockSpec(memory_space=pltpu.HBM)
WHOLE = pl.BlockSpec(memory_space=pltpu.VMEM)


def run_copies(copies):
    for copy in copies:
        copy.start()
    for copy in copies:
        copy.wait()


def head_columns(owner, local_width, first, width):
    return pl.ds(pl.multiple_of(owner * local_width + first, 128), width)


def flipped(k, shards):
    bits = shards.bit_length() - 1
    if bits % 2:
        return k
    low = (1 << bits // 2) - 1
    return (k & low) << bits // 2 | k >> bits // 2


def partner_of(k, shards):
    odd = lax.axis_index("dp") & 1
    return lax.axis_index("seq") ^ (k + odd * (flipped(k, shards) - k))


def pack_kernel(shards, local_width, first, width, *refs):
    rows, outs, sems = refs[:4], refs[4:-1], refs[-1]
    run_copies(
        [
            pltpu.make_async_copy(
                rows[a].at[0, :, head_columns(partner_of(k, shards), local_width, first, width)],
                out.at[a],
                sems.at[k, a],
            )
            for k, out in enumerate(outs, start=1)
            for a in range(4)
        ]
    )


def pack(shards, local_width, first, width, rows):
    shape = jax.ShapeDtypeStruct((4, rows[0].shape[1], width), rows[0].dtype)
    moved = (shards - 1) * math.prod(shape.shape) * 4
    return pl.pallas_call(
        functools.partial(pack_kernel, shards, local_width, first, width),
        out_shape=[shape] * (shards - 1),
        in_specs=[HBM] * 4,
        out_specs=[ANY] * (shards - 1),
        scratch_shapes=[pltpu.SemaphoreType.DMA((shards, 4))],
        compiler_params=pltpu.CompilerParams(vmem_limit_bytes=VMEM_LIMIT),
        cost_estimate=pl.CostEstimate(flops=0, bytes_accessed=moved, transcendentals=0),
        name="pack",
    )(*rows)


def unpack_kernel(shards, local_width, first, width, held, *refs):
    pieces, outs, sems = refs[:shards], refs[shards + held : -1], refs[-1]
    run_copies(
        [
            pltpu.make_async_copy(
                pieces[k].at[a],
                outs[a].at[0, :, head_columns(partner_of(k, shards), local_width, first, width)],
                sems.at[k, a],
            )
            for k in range(shards)
            for a in range(4)
        ]
    )


def unpack(shards, local_width, first, width, pieces, held):
    tokens = pieces[0].shape[1]
    shape = jax.ShapeDtypeStruct((1, tokens, shards * local_width), pieces[0].dtype)
    moved = sum(piece.size for piece in pieces) * 4
    return pl.pallas_call(
        functools.partial(unpack_kernel, shards, local_width, first, width, len(held)),
        out_shape=[shape] * 4,
        in_specs=[ANY] * (shards + len(held)),
        out_specs=[ANY] * 4,
        input_output_aliases={shards + a: a for a in range(len(held))},
        scratch_shapes=[pltpu.SemaphoreType.DMA((shards, 4))],
        compiler_params=pltpu.CompilerParams(vmem_limit_bytes=VMEM_LIMIT),
        cost_estimate=pl.CostEstimate(flops=0, bytes_accessed=moved, transcendentals=0),
        name="unpack",
    )(*pieces, *held)


def dot_nn(left, right):
    return lax.dot_general(
        left, right, (((1,), (0,)), ((), ())), preferred_element_type=jnp.float32
    )


def dot_nt(left, right):
    return lax.dot_general(
        left, right, (((1,), (1,)), ((), ())), preferred_element_type=jnp.float32
    )


def dot_tn(left, right):
    return lax.dot_general(
        left, right, (((0,), (0,)), ((), ())), preferred_element_type=jnp.float32
    )


def norm_forward(rows, gain):
    inverse = lax.rsqrt(jnp.mean(rows * rows, axis=1, keepdims=True) + EPSILON)
    unit = rows * inverse
    return (unit * gain).astype(jnp.bfloat16), unit, inverse


def norm_backward(grads, unit, inverse, gain, score_scale):
    scaled = grads * (gain * score_scale)
    along = jnp.mean(scaled * unit, axis=1, keepdims=True)
    gain_grad = jnp.sum(grads * unit, axis=0, keepdims=True) * score_scale
    return inverse * (scaled - unit * along), gain_grad


def attend(queries, keys, values, grads, gain_q, gain_k, allowed, block, score_scale):
    query_norm, query_unit, query_inverse = norm_forward(queries, gain_q)
    key_norm, key_unit, key_inverse = norm_forward(keys, gain_k)
    values = values.astype(jnp.bfloat16)
    grads = grads.astype(jnp.bfloat16)
    outs, query_grads = [], []
    key_grad = value_grad = None
    exponent_scale = score_scale * math.log2(math.e)
    for start in range(0, queries.shape[0], block):
        rows = slice(start, start + block)
        query_block, grads_block = query_norm[rows], grads[rows]
        scores = dot_nt(key_norm, query_block)
        if allowed is not None:
            scores = jnp.where(allowed, scores, NEGATIVE)
        row_max = jnp.max(scores, axis=0, keepdims=True)
        shifted = jnp.exp2((scores - row_max) * exponent_scale)
        if allowed is not None:
            shifted = jnp.where(allowed, shifted, 0.0)
        weights = shifted * (1.0 / jnp.sum(shifted, axis=0, keepdims=True))
        weights_low = weights.astype(jnp.bfloat16)
        output = dot_tn(values, weights_low)
        grads_turned = grads_block.astype(jnp.float32).T
        row_delta = jnp.sum(grads_turned * output, axis=0, keepdims=True)
        grad_probs = dot_nt(values, grads_block)
        grad_scores = (weights * (grad_probs - row_delta)).astype(jnp.bfloat16)
        outs.append(output.T)
        query_grads.append(dot_tn(key_norm, grad_scores).T)
        value_part = dot_nn(weights_low, grads_block)
        key_part = dot_nn(grad_scores, query_block)
        value_grad = value_part if value_grad is None else value_grad + value_part
        key_grad = key_part if key_grad is None else key_grad + key_part
    join = lambda parts: parts[0] if len(parts) == 1 else jnp.concatenate(parts, axis=0)
    query_grad, gain_grad_q = norm_backward(
        join(query_grads), query_unit, query_inverse, gain_q, score_scale
    )
    key_grad, gain_grad_k = norm_backward(key_grad, key_unit, key_inverse, gain_k, score_scale)
    return (join(outs), query_grad, key_grad, value_grad), (gain_grad_q, gain_grad_k)


def attention_kernel(shards, first, heads, has_held, *refs):
    own, refs = refs[:4], refs[4:]
    received, refs = refs[: shards - 1], refs[shards - 1 :]
    (seg_ref, gain_q_ref, gain_k_ref), refs = refs[:3], refs[3:]
    if has_held:
        held_ref, refs = refs[0], refs[1:]
    sent, refs = refs[:shards], refs[shards:]
    gains_ref, inputs, results, in_sems, out_sems = refs
    me = lax.axis_index("seq")
    tokens, head_dim = own[0].shape[1], gain_q_ref.shape[1]
    local_width = gain_q_ref.shape[0] * head_dim
    width = heads * head_dim
    length = shards * tokens
    quarter = length // 4
    score_scale = 1.0 / math.sqrt(head_dim)

    def place(k):
        return pl.ds(pl.multiple_of(partner_of(k, shards) * tokens, tokens), tokens)

    own_columns = head_columns(me, local_width, first * head_dim, width)
    copies = [
        pltpu.make_async_copy(
            own[a].at[0, :, own_columns], inputs.at[a, place(0), :], in_sems.at[0, a]
        )
        for a in range(4)
    ]
    copies += [
        pltpu.make_async_copy(
            received[k - 1].at[a], inputs.at[a, place(k), :], in_sems.at[k, a]
        )
        for k in range(1, shards)
        for a in range(4)
    ]
    for copy in copies:
        copy.start()

    segments = seg_ref[...].astype(jnp.float32)
    lane = lax.broadcasted_iota(jnp.int32, (1, length), 1)
    middle = jnp.max(jnp.where(lane == length // 2, segments, -1.0), axis=1, keepdims=True)
    before = jnp.sum(jnp.where(segments < middle, 1.0, 0.0), axis=1, keepdims=True)
    row = lax.broadcasted_iota(jnp.int32, (quarter, head_dim), 0).astype(jnp.float32)
    late = row >= before
    late_lanes = lane[:, :quarter].astype(jnp.float32) >= before
    seg_rest = jnp.where(late_lanes, segments[:, 3 * quarter :], segments[:, :quarter])
    seg_lanes = jnp.broadcast_to(seg_rest, (quarter, quarter))
    allowed = seg_lanes == seg_lanes.T

    for copy in copies:
        copy.wait()

    for head in range(heads):
        columns = slice(head * head_dim, (head + 1) * head_dim)
        image, rest = [], []
        for a in range(4):
            early = inputs[a, :quarter, columns].astype(jnp.float32)
            latest = inputs[a, 3 * quarter :, columns].astype(jnp.float32)
            middle_rows = inputs[a, quarter : 3 * quarter, columns].astype(jnp.float32)
            image.append(jnp.concatenate([jnp.where(late, early, latest), middle_rows], axis=0))
            rest.append(jnp.where(late, latest, early))
        gain_q = gain_q_ref[first + head : first + head + 1, :]
        gain_k = gain_k_ref[first + head : first + head + 1, :]
        block = min(3 * quarter, 384)
        image_out, image_gains = attend(*image, gain_q, gain_k, None, block, score_scale)
        rest_out, rest_gains = attend(*rest, gain_q, gain_k, allowed, quarter, score_scale)
        for a in range(4):
            shared, other = image_out[a][:quarter], rest_out[a]
            results[a, :quarter, columns] = jnp.where(late, shared, other).astype(jnp.bfloat16)
            results[a, quarter : 3 * quarter, columns] = image_out[a][quarter:].astype(jnp.bfloat16)
            results[a, 3 * quarter :, columns] = jnp.where(late, other, shared).astype(jnp.bfloat16)
        for side in range(2):
            gains_ref[side, first + head : first + head + 1, :] = image_gains[side] + rest_gains[side]
    if has_held:
        gains_ref[:, :first, :] = held_ref[:, :first, :]

    run_copies(
        [
            pltpu.make_async_copy(
                results.at[a, place(k), :], sent[k].at[a], out_sems.at[k, a]
            )
            for k in range(shards)
            for a in range(4)
        ]
    )


def attention(shards, first, heads, rows, received, segments, gain_q, gain_k, held):
    tokens, head_dim = rows[0].shape[1], gain_q.shape[1]
    width, length = heads * head_dim, shards * tokens
    pieces = [jax.ShapeDtypeStruct((4, tokens, width), jnp.bfloat16)] * shards
    gains = jax.ShapeDtypeStruct((2,) + gain_q.shape, jnp.float32)
    cost = pl.CostEstimate(
        flops=12 * heads * length * length * head_dim,
        bytes_accessed=16 * length * width,
        transcendentals=heads * length * length,
    )
    return pl.pallas_call(
        functools.partial(attention_kernel, shards, first, heads, len(held) > 0),
        out_shape=pieces + [gains],
        in_specs=[HBM] * 4 + [ANY] * len(received) + [WHOLE] * (3 + len(held)),
        out_specs=[ANY] * len(pieces) + [WHOLE],
        scratch_shapes=[
            pltpu.VMEM((4, length, width), jnp.bfloat16),
            pltpu.VMEM((4, length, width), jnp.bfloat16),
            pltpu.SemaphoreType.DMA((shards, 4)),
            pltpu.SemaphoreType.DMA((shards, 4)),
        ],
        compiler_params=pltpu.CompilerParams(vmem_limit_bytes=VMEM_LIMIT),
        cost_estimate=cost,
        name="attention",
    )(*rows, *received, segments, gain_q, gain_k, *held)


def exchange(array, axis, size, k):
    return lax.ppermute(array, axis, [(i, i ^ k) for i in range(size)])


def exchange_slots(pieces, packs, shards):
    arrived = []
    for k, piece in enumerate(pieces, start=1):
        pairs = [
            (pack * shards + i, pack * shards + (i ^ (flipped(k, shards) if pack % 2 else k)))
            for pack in range(packs)
            for i in range(shards)
        ]
        arrived.append(lax.ppermute(piece, ("dp", "seq"), pairs))
    return arrived


def on_device(shards, packs, query_rows, key_rows, value_rows, out_cotangent, segment_ids, gain_query, gain_key):
    rows = tuple(
        pltpu.with_memory_space_constraint(array, pltpu.HBM)
        for array in (query_rows, key_rows, value_rows, out_cotangent)
    )
    local_heads, head_dim = gain_query.shape
    local_width = local_heads * head_dim
    heads = local_heads // 2 if local_heads % 2 == 0 else local_heads
    firsts = range(0, local_heads, heads)
    width = heads * head_dim
    arrived = []
    for first in firsts:
        packed = pack(shards, local_width, first * head_dim, width, rows)
        arrived.append(exchange_slots(packed, packs, shards))
    gains = ()
    returned = []
    for first, received in zip(firsts, arrived):
        *pieces, gains = attention(
            shards, first, heads, rows, received, segment_ids, gain_query, gain_key, gains
        )
        gains = (gains,)
        returned.append(pieces[:1] + exchange_slots(pieces[1:], packs, shards))
    total, step = gains[0], 1
    while step < packs:
        waited = slice(0, -1) if step == 1 else slice(-1, None)
        if step <= 2:
            total, returned[0][waited] = lax.optimization_barrier((total, returned[0][waited]))
        total = total + exchange(total, "dp", packs, step)
        step *= 2
    sums = (total[0], total[1])
    sums, returned[-1][0] = lax.optimization_barrier((sums, returned[-1][0]))
    outs = ()
    for first, pieces in zip(firsts, returned):
        outs = unpack(shards, local_width, first * head_dim, width, pieces, outs)
    return (*outs, *sums)


def solution(mesh):
    rows = P("dp", "seq", None)
    gain = P("seq", None)
    return jax.shard_map(
        functools.partial(on_device, mesh.shape["seq"], mesh.shape["dp"]),
        mesh=mesh,
        in_specs=(rows, rows, rows, rows, P("dp", None), gain, gain),
        out_specs=(rows, rows, rows, rows, gain, gain),
        check_vma=False,
    )
```

profile of v0, /device:TPU:0, one launch (start us, length us, event | category | flops | bytes accessed | tf_op | source)
XLA Modules:
  0.0 53.0 jit_solution(317156277755565315)
XLA Ops:
  0.6 1.3 %pack.3 = (bf16[4,128,256]{2,1,0:T(8,128)(2,1)S(1)}, bf16[4,128,256]{2,1,0:T(8,128)(2,1)S(1)}, bf16[4,128,256]{2,1,0:T(8,128)(2,1)S(1)}) custom-call(bf16[1,128,2048]{2,1,0:T(8,128)(2,1)} %refs_0_.7, bf16[1,128,2048]{2,1,0:T(8,128)(2,1)} %refs_1_.7, bf16[1,128,2048]{2,1,0:T(8,128)(2,1)} %refs_2_.7, bf16[1,128,2048]{2,1,0:T(8,128)(2,1)} %refs_3_.7), custom_call_target="tpu_custom_call" | custom-call | bytes 1572864 | tf_op jit(solution)/shard_map/pack/pallas_call | solution.py:61
  2.0 3.0 %collective-permute-start.3 = (bf16[4,128,256]{2,1,0:T(8,128)(2,1)S(1)}, bf16[4,128,256]{2,1,0:T(8,128)(2,1)S(1)}, u32[]{:S(2)}, u32[]{:S(2)}) collective-permute-start(bf16[4,128,256]{2,1,0:T(8,128)(2,1)S(1)} %get-tuple-element.42), channel_id=1, source_target_pairs={{0,1},{1,0},{2,3},{3,2},{4,6},{5,7},{6,4},{7,5},{8,9},{9,8},{10,11... | collective-permute-start | bytes 786440 | tf_op jit(solution)/shard_map/ppermute | solution.py:299
  5.0 1.5 %collective-permute-start.4 = (bf16[4,128,256]{2,1,0:T(8,128)(2,1)S(1)}, bf16[4,128,256]{2,1,0:T(8,128)(2,1)S(1)}, u32[]{:S(2)}, u32[]{:S(2)}) collective-permute-start(bf16[4,128,256]{2,1,0:T(8,128)(2,1)S(1)} %get-tuple-element.43), channel_id=1, source_target_pairs={{0,2},{1,3},{2,0},{3,1},{4,5},{5,4},{6,7},{7,6},{8,10},{9,11},{10,... | collective-permute-start | bytes 786440 | tf_op jit(solution)/shard_map/ppermute | solution.py:299
  6.5 0.0 collective-permute-start.5
  6.5 1.3 %pack.2 = (bf16[4,128,256]{2,1,0:T(8,128)(2,1)S(1)}, bf16[4,128,256]{2,1,0:T(8,128)(2,1)S(1)}, bf16[4,128,256]{2,1,0:T(8,128)(2,1)S(1)}) custom-call(bf16[1,128,2048]{2,1,0:T(8,128)(2,1)} %refs_0_.7, bf16[1,128,2048]{2,1,0:T(8,128)(2,1)} %refs_1_.7, bf16[1,128,2048]{2,1,0:T(8,128)(2,1)} %refs_2_.7, bf16[1,128,2048]{2,1,0:T(8,128)(2,1)} %refs_3_.7), custom_call_target="tpu_custom_call" | custom-call | bytes 1572864 | tf_op jit(solution)/shard_map/pack/pallas_call | solution.py:61
  7.8 0.0 copy-start.1
  7.8 0.0 copy-start
  7.9 2.0 %collective-permute-start = (bf16[4,128,256]{2,1,0:T(8,128)(2,1)S(1)}, bf16[4,128,256]{2,1,0:T(8,128)(2,1)S(1)}, u32[]{:S(2)}, u32[]{:S(2)}) collective-permute-start(bf16[4,128,256]{2,1,0:T(8,128)(2,1)S(1)} %get-tuple-element.39), channel_id=1, source_target_pairs={{0,1},{1,0},{2,3},{3,2},{4,6},{5,7},{6,4},{7,5},{8,9},{9,8},{10,11... | collective-permute-start | bytes 786440 | tf_op jit(solution)/shard_map/ppermute | solution.py:299
  9.9 1.5 %collective-permute-start.1 = (bf16[4,128,256]{2,1,0:T(8,128)(2,1)S(1)}, bf16[4,128,256]{2,1,0:T(8,128)(2,1)S(1)}, u32[]{:S(2)}, u32[]{:S(2)}) collective-permute-start(bf16[4,128,256]{2,1,0:T(8,128)(2,1)S(1)} %get-tuple-element.40), channel_id=1, source_target_pairs={{0,2},{1,3},{2,0},{3,1},{4,5},{5,4},{6,7},{7,6},{8,10},{9,11},{10,... | collective-permute-start | bytes 786440 | tf_op jit(solution)/shard_map/ppermute | solution.py:299
  11.4 0.2 collective-permute-done.3.refs_4_
  11.6 3.5 %collective-permute-start.2 = (bf16[4,128,256]{2,1,0:T(8,128)(2,1)S(1)}, bf16[4,128,256]{2,1,0:T(8,128)(2,1)S(1)}, u32[]{:S(2)}, u32[]{:S(2)}) collective-permute-start(bf16[4,128,256]{2,1,0:T(8,128)(2,1)S(1)} %get-tuple-element.41), channel_id=1, source_target_pairs={{0,3},{1,2},{2,1},{3,0},{4,7},{5,6},{6,5},{7,4},{8,11},{9,10},{10,... | collective-permute-start | bytes 786440 | tf_op jit(solution)/shard_map/ppermute | solution.py:299
  15.1 2.5 %collective-permute-done.4.refs_5_ = bf16[4,128,256]{2,1,0:T(8,128)(2,1)S(1)} collective-permute-done((bf16[4,128,256]{2,1,0:T(8,128)(2,1)S(1)}, bf16[4,128,256]{2,1,0:T(8,128)(2,1)S(1)}, u32[]{:S(2)}, u32[]{:S(2)}) %collective-permute-start.4) | collective-permute-done | bytes 262176 | tf_op jit(solution)/shard_map/ppermute | solution.py:299
  17.6 1.7 %collective-permute-done.5.refs_6_ = bf16[4,128,256]{2,1,0:T(8,128)(2,1)S(1)} collective-permute-done((bf16[4,128,256]{2,1,0:T(8,128)(2,1)S(1)}, bf16[4,128,256]{2,1,0:T(8,128)(2,1)S(1)}, u32[]{:S(2)}, u32[]{:S(2)}) %collective-permute-start.5) | collective-permute-done | bytes 262176 | tf_op jit(solution)/shard_map/ppermute | solution.py:299
  19.3 6.3 %attention.2 = (bf16[4,128,256]{2,1,0:T(8,128)(2,1)S(1)}, bf16[4,128,256]{2,1,0:T(8,128)(2,1)S(1)}, bf16[4,128,256]{2,1,0:T(8,128)(2,1)S(1)}, bf16[4,128,256]{2,1,0:T(8,128)(2,1)S(1)}, f32[2,4,128]{2,1,0:T(4,128)S(1)}) custom-call(bf16[1,128,2048]{2,1,0:T(8,128)(2,1)} %refs_0_.7, bf16[1,128,2048]{2,1,0:T(8,128)(2,1)} %refs_1_.7, ...), custom_call_target="tpu_custom_call" | custom-call | flops 805306368 | bytes 2097152 | tf_op jit(solution)/shard_map/attention/pallas_call | solution.py:270
  25.6 1.6 %collective-permute-start.6 = (bf16[4,128,256]{2,1,0:T(8,128)(2,1)S(1)}, bf16[4,128,256]{2,1,0:T(8,128)(2,1)S(1)}, u32[]{:S(2)}, u32[]{:S(2)}) collective-permute-start(bf16[4,128,256]{2,1,0:T(8,128)(2,1)S(1)} %get-tuple-element.48), channel_id=1, source_target_pairs={{0,1},{1,0},{2,3},{3,2},{4,6},{5,7},{6,4},{7,5},{8,9},{9,8},{10,11... | collective-permute-start | bytes 786440 | tf_op jit(solution)/shard_map/ppermute | solution.py:299
  27.2 0.9 %collective-permute-start.7 = (bf16[4,128,256]{2,1,0:T(8,128)(2,1)S(1)}, bf16[4,128,256]{2,1,0:T(8,128)(2,1)S(1)}, u32[]{:S(2)}, u32[]{:S(2)}) collective-permute-start(bf16[4,128,256]{2,1,0:T(8,128)(2,1)S(1)} %get-tuple-element.49), channel_id=1, source_target_pairs={{0,2},{1,3},{2,0},{3,1},{4,5},{5,4},{6,7},{7,6},{8,10},{9,11},{10,... | collective-permute-start | bytes 786440 | tf_op jit(solution)/shard_map/ppermute | solution.py:299
  28.1 1.1 %collective-permute-start.9 = (bf16[4,128,256]{2,1,0:T(8,128)(2,1)S(1)}, bf16[4,128,256]{2,1,0:T(8,128)(2,1)S(1)}, u32[]{:S(2)}, u32[]{:S(2)}) collective-permute-start(bf16[4,128,256]{2,1,0:T(8,128)(2,1)S(1)} %get-tuple-element.51), channel_id=1, source_target_pairs={{0,3},{1,2},{2,1},{3,0},{4,7},{5,6},{6,5},{7,4},{8,11},{9,10},{10,... | collective-permute-start | bytes 786440 | tf_op jit(solution)/shard_map/ppermute | solution.py:299
  29.2 1.3 %collective-permute-done.2.refs_6_ = bf16[4,128,256]{2,1,0:T(8,128)(2,1)S(1)} collective-permute-done((bf16[4,128,256]{2,1,0:T(8,128)(2,1)S(1)}, bf16[4,128,256]{2,1,0:T(8,128)(2,1)S(1)}, u32[]{:S(2)}, u32[]{:S(2)}) %collective-permute-start.2) | collective-permute-done | bytes 262176 | tf_op jit(solution)/shard_map/ppermute | solution.py:299
  30.5 6.3 %attention.3 = (bf16[4,128,256]{2,1,0:T(8,128)(2,1)S(1)}, bf16[4,128,256]{2,1,0:T(8,128)(2,1)S(1)}, bf16[4,128,256]{2,1,0:T(8,128)(2,1)S(1)}, bf16[4,128,256]{2,1,0:T(8,128)(2,1)S(1)}, f32[2,4,128]{2,1,0:T(4,128)S(1)}) custom-call(bf16[1,128,2048]{2,1,0:T(8,128)(2,1)} %refs_0_.7, bf16[1,128,2048]{2,1,0:T(8,128)(2,1)} %refs_1_.7, ...), custom_call_target="tpu_custom_call" | custom-call | flops 805306368 | bytes 2097152 | tf_op jit(solution)/shard_map/attention/pallas_call | solution.py:270
  36.8 1.6 %collective-permute-start.12 = (bf16[4,128,256]{2,1,0:T(8,128)(2,1)S(1)}, bf16[4,128,256]{2,1,0:T(8,128)(2,1)S(1)}, u32[]{:S(2)}, u32[]{:S(2)}) collective-permute-start(bf16[4,128,256]{2,1,0:T(8,128)(2,1)S(1)} %get-tuple-element.55), channel_id=1, source_target_pairs={{0,1},{1,0},{2,3},{3,2},{4,6},{5,7},{6,4},{7,5},{8,9},{9,8},{10,11... | collective-permute-start | bytes 786440 | tf_op jit(solution)/shard_map/ppermute | solution.py:299
  38.4 0.5 collective-permute-start.13
  38.9 1.5 %collective-permute-start.14 = (bf16[4,128,256]{2,1,0:T(8,128)(2,1)S(1)}, bf16[4,128,256]{2,1,0:T(8,128)(2,1)S(1)}, u32[]{:S(2)}, u32[]{:S(2)}) collective-permute-start(bf16[4,128,256]{2,1,0:T(8,128)(2,1)S(1)} %get-tuple-element.57), channel_id=1, source_target_pairs={{0,3},{1,2},{2,1},{3,0},{4,7},{5,6},{6,5},{7,4},{8,11},{9,10},{10,... | collective-permute-start | bytes 786440 | tf_op jit(solution)/shard_map/ppermute | solution.py:299
  40.4 1.2 %collective-permute-done.8 = f32[2,4,128]{2,1,0:T(4,128)S(1)} collective-permute-done((f32[2,4,128]{2,1,0:T(4,128)S(1)}, f32[2,4,128]{2,1,0:T(4,128)S(1)}, u32[]{:S(2)}, u32[]{:S(2)}) %collective-permute-start.8) | collective-permute-done | bytes 4128 | tf_op jit(solution)/shard_map/ppermute | solution.py:288
  41.5 0.2 collective-permute-done.9.refs_3_
  41.8 1.5 %collective-permute-start.10 = (f32[2,4,128]{2,1,0:T(4,128)S(1)}, f32[2,4,128]{2,1,0:T(4,128)S(1)}, u32[]{:S(2)}, u32[]{:S(2)}) collective-permute-start(f32[2,4,128]{2,1,0:T(4,128)S(1)} %add.9), channel_id=1, source_target_pairs={{0,8},{4,12},{8,0},{12,4},{16,24},{20,28},{24,16},{28,20},{1,9},{5... | collective-permute-start | bytes 12296 | tf_op jit(solution)/shard_map/ppermute | solution.py:288
  43.3 2.1 %collective-permute-done.10 = f32[2,4,128]{2,1,0:T(4,128)S(1)} collective-permute-done((f32[2,4,128]{2,1,0:T(4,128)S(1)}, f32[2,4,128]{2,1,0:T(4,128)S(1)}, u32[]{:S(2)}, u32[]{:S(2)}) %collective-permute-start.10) | collective-permute-done | bytes 4128 | tf_op jit(solution)/shard_map/ppermute | solution.py:288
  45.4 2.6 %collective-permute-start.11 = (f32[2,4,128]{2,1,0:T(4,128)S(1)}, f32[2,4,128]{2,1,0:T(4,128)S(1)}, u32[]{:S(2)}, u32[]{:S(2)}) collective-permute-start(f32[2,4,128]{2,1,0:T(4,128)S(1)} %add.10), channel_id=1, source_target_pairs={{0,16},{4,20},{8,24},{12,28},{16,0},{20,4},{24,8},{28,12},{1,17},{... | collective-permute-start | bytes 12296 | tf_op jit(solution)/shard_map/ppermute | solution.py:288
  48.0 1.1 %unpack.2 = (bf16[1,128,2048]{2,1,0:T(8,128)(2,1)}, bf16[1,128,2048]{2,1,0:T(8,128)(2,1)}, bf16[1,128,2048]{2,1,0:T(8,128)(2,1)}, bf16[1,128,2048]{2,1,0:T(8,128)(2,1)}) custom-call(bf16[4,128,256]{2,1,0:T(8,128)(2,1)S(1)} %get-tuple-element.58.refs_0_, bf16[4,128,256]{2,1,0:T(8,128)(2,1)S(1)} %collective-permute-done.6.refs_1_, ...), custom_call_target="tpu_custom_call" | custom-call | bytes 2097152 | tf_op jit(solution)/shard_map/unpack/pallas_call | solution.py:92
  49.1 0.8 %collective-permute-done.11 = f32[2,4,128]{2,1,0:T(4,128)S(1)} collective-permute-done((f32[2,4,128]{2,1,0:T(4,128)S(1)}, f32[2,4,128]{2,1,0:T(4,128)S(1)}, u32[]{:S(2)}, u32[]{:S(2)}) %collective-permute-start.11) | collective-permute-done | bytes 4128 | tf_op jit(solution)/shard_map/ppermute | solution.py:288
  49.9 0.6 %slice_bitcast_fusion = (f32[4,128]{1,0:T(4,128)}, f32[4,128]{1,0:T(4,128)}) fusion(f32[2,4,128]{2,1,0:T(4,128)S(1)} %add.11), kind=kLoop, calls=%fused_computation | loop fusion | bytes 8192 | tf_op jit(solution)/shard_map/squeeze | solution.py:332
  50.5 1.5 %collective-permute-done.14.refs_3_ = bf16[4,128,256]{2,1,0:T(8,128)(2,1)S(1)} collective-permute-done((bf16[4,128,256]{2,1,0:T(8,128)(2,1)S(1)}, bf16[4,128,256]{2,1,0:T(8,128)(2,1)S(1)}, u32[]{:S(2)}, u32[]{:S(2)}) %collective-permute-start.14) | collective-permute-done | bytes 262176 | tf_op jit(solution)/shard_map/ppermute | solution.py:299
  52.0 1.1 %unpack.3 = (bf16[1,128,2048]{2,1,0:T(8,128)(2,1)}, bf16[1,128,2048]{2,1,0:T(8,128)(2,1)}, bf16[1,128,2048]{2,1,0:T(8,128)(2,1)}, bf16[1,128,2048]{2,1,0:T(8,128)(2,1)}) custom-call(bf16[4,128,256]{2,1,0:T(8,128)(2,1)S(1)} %get-tuple-element.54.refs_0_, ...), custom_call_target="tpu_custom_call", output_to_operand_aliasing={{0}: (4, {}), {1}: (5, {}), {2}: (6, {}), {3}: (7, {})} | custom-call | bytes 2097152 | tf_op jit(solution)/shard_map/unpack/pallas_call | solution.py:92
  (14 shorter events, 0.0 us)
Async XLA Ops:
  2.0 9.6 %collective-permute-start.3 = (bf16[4,128,256]{2,1,0:T(8,128)(2,1)S(1)}, bf16[4,128,256]{2,1,0:T(8,128)(2,1)S(1)}, u32[]{:S(2)}, u32[]{:S(2)}) collective-permute-start(bf16[4,128,256]{2,1,0:T(8,128)(2,1)S(1)} %get-tuple-element.42), channel_id=1, source_target_pairs={{0,1},{1,0},{2,3},{3,2},{4,6},{5,7},{6,4},{7,5},{8,9},{9,8},{10,11... | collective-permute-start | bytes 786440 | tf_op jit(solution)/shard_map/ppermute | solution.py:299
  5.0 12.6 %collective-permute-start.4 = (bf16[4,128,256]{2,1,0:T(8,128)(2,1)S(1)}, bf16[4,128,256]{2,1,0:T(8,128)(2,1)S(1)}, u32[]{:S(2)}, u32[]{:S(2)}) collective-permute-start(bf16[4,128,256]{2,1,0:T(8,128)(2,1)S(1)} %get-tuple-element.43), channel_id=1, source_target_pairs={{0,2},{1,3},{2,0},{3,1},{4,5},{5,4},{6,7},{7,6},{8,10},{9,11},{10,... | collective-permute-start | bytes 786440 | tf_op jit(solution)/shard_map/ppermute | solution.py:299
  6.5 12.8 %collective-permute-start.5 = (bf16[4,128,256]{2,1,0:T(8,128)(2,1)S(1)}, bf16[4,128,256]{2,1,0:T(8,128)(2,1)S(1)}, u32[]{:S(2)}, u32[]{:S(2)}) collective-permute-start(bf16[4,128,256]{2,1,0:T(8,128)(2,1)S(1)} %get-tuple-element.44), channel_id=1, source_target_pairs={{0,3},{1,2},{2,1},{3,0},{4,7},{5,6},{6,5},{7,4},{8,11},{9,10},{10,... | collective-permute-start | bytes 786440 | tf_op jit(solution)/shard_map/ppermute | solution.py:299
  6.5 12.8 %copy-start.2 = (f32[4,128]{1,0:T(4,128)S(1)}, f32[4,128]{1,0:T(4,128)}, u32[]{:S(2)}) copy-start(f32[4,128]{1,0:T(4,128)} %refs_9_.3) | copy-start | bytes 6148
  7.8 11.4 %copy-start.1 = (f32[4,128]{1,0:T(4,128)S(1)}, f32[4,128]{1,0:T(4,128)}, u32[]{:S(2)}) copy-start(f32[4,128]{1,0:T(4,128)} %refs_8_.3) | copy-start | bytes 6148
  7.8 11.4 %copy-start = (s32[1,512]{1,0:T(1,128)S(1)}, s32[1,512]{1,0:T(1,128)}, u32[]{:S(2)}) copy-start(s32[1,512]{1,0:T(1,128)} %refs_7_.3) | copy-start | bytes 6148
  7.9 20.2 %collective-permute-start = (bf16[4,128,256]{2,1,0:T(8,128)(2,1)S(1)}, bf16[4,128,256]{2,1,0:T(8,128)(2,1)S(1)}, u32[]{:S(2)}, u32[]{:S(2)}) collective-permute-start(bf16[4,128,256]{2,1,0:T(8,128)(2,1)S(1)} %get-tuple-element.39), channel_id=1, source_target_pairs={{0,1},{1,0},{2,3},{3,2},{4,6},{5,7},{6,4},{7,5},{8,9},{9,8},{10,11... | collective-permute-start | bytes 786440 | tf_op jit(solution)/shard_map/ppermute | solution.py:299
  9.9 19.3 %collective-permute-start.1 = (bf16[4,128,256]{2,1,0:T(8,128)(2,1)S(1)}, bf16[4,128,256]{2,1,0:T(8,128)(2,1)S(1)}, u32[]{:S(2)}, u32[]{:S(2)}) collective-permute-start(bf16[4,128,256]{2,1,0:T(8,128)(2,1)S(1)} %get-tuple-element.40), channel_id=1, source_target_pairs={{0,2},{1,3},{2,0},{3,1},{4,5},{5,4},{6,7},{7,6},{8,10},{9,11},{10,... | collective-permute-start | bytes 786440 | tf_op jit(solution)/shard_map/ppermute | solution.py:299
  11.6 19.0 %collective-permute-start.2 = (bf16[4,128,256]{2,1,0:T(8,128)(2,1)S(1)}, bf16[4,128,256]{2,1,0:T(8,128)(2,1)S(1)}, u32[]{:S(2)}, u32[]{:S(2)}) collective-permute-start(bf16[4,128,256]{2,1,0:T(8,128)(2,1)S(1)} %get-tuple-element.41), channel_id=1, source_target_pairs={{0,3},{1,2},{2,1},{3,0},{4,7},{5,6},{6,5},{7,4},{8,11},{9,10},{10,... | collective-permute-start | bytes 786440 | tf_op jit(solution)/shard_map/ppermute | solution.py:299
  25.6 13.2 %collective-permute-start.6 = (bf16[4,128,256]{2,1,0:T(8,128)(2,1)S(1)}, bf16[4,128,256]{2,1,0:T(8,128)(2,1)S(1)}, u32[]{:S(2)}, u32[]{:S(2)}) collective-permute-start(bf16[4,128,256]{2,1,0:T(8,128)(2,1)S(1)} %get-tuple-element.48), channel_id=1, source_target_pairs={{0,1},{1,0},{2,3},{3,2},{4,6},{5,7},{6,4},{7,5},{8,9},{9,8},{10,11... | collective-permute-start | bytes 786440 | tf_op jit(solution)/shard_map/ppermute | solution.py:299
  27.2 13.2 %collective-permute-start.7 = (bf16[4,128,256]{2,1,0:T(8,128)(2,1)S(1)}, bf16[4,128,256]{2,1,0:T(8,128)(2,1)S(1)}, u32[]{:S(2)}, u32[]{:S(2)}) collective-permute-start(bf16[4,128,256]{2,1,0:T(8,128)(2,1)S(1)} %get-tuple-element.49), channel_id=1, source_target_pairs={{0,2},{1,3},{2,0},{3,1},{4,5},{5,4},{6,7},{7,6},{8,10},{9,11},{10,... | collective-permute-start | bytes 786440 | tf_op jit(solution)/shard_map/ppermute | solution.py:299
  28.1 13.7 %collective-permute-start.9 = (bf16[4,128,256]{2,1,0:T(8,128)(2,1)S(1)}, bf16[4,128,256]{2,1,0:T(8,128)(2,1)S(1)}, u32[]{:S(2)}, u32[]{:S(2)}) collective-permute-start(bf16[4,128,256]{2,1,0:T(8,128)(2,1)S(1)} %get-tuple-element.51), channel_id=1, source_target_pairs={{0,3},{1,2},{2,1},{3,0},{4,7},{5,6},{6,5},{7,4},{8,11},{9,10},{10,... | collective-permute-start | bytes 786440 | tf_op jit(solution)/shard_map/ppermute | solution.py:299
  36.8 13.7 %collective-permute-start.12 = (bf16[4,128,256]{2,1,0:T(8,128)(2,1)S(1)}, bf16[4,128,256]{2,1,0:T(8,128)(2,1)S(1)}, u32[]{:S(2)}, u32[]{:S(2)}) collective-permute-start(bf16[4,128,256]{2,1,0:T(8,128)(2,1)S(1)} %get-tuple-element.55), channel_id=1, source_target_pairs={{0,1},{1,0},{2,3},{3,2},{4,6},{5,7},{6,4},{7,5},{8,9},{9,8},{10,11... | collective-permute-start | bytes 786440 | tf_op jit(solution)/shard_map/ppermute | solution.py:299
  38.4 12.1 %collective-permute-start.13 = (bf16[4,128,256]{2,1,0:T(8,128)(2,1)S(1)}, bf16[4,128,256]{2,1,0:T(8,128)(2,1)S(1)}, u32[]{:S(2)}, u32[]{:S(2)}) collective-permute-start(bf16[4,128,256]{2,1,0:T(8,128)(2,1)S(1)} %get-tuple-element.56), channel_id=1, source_target_pairs={{0,2},{1,3},{2,0},{3,1},{4,5},{5,4},{6,7},{7,6},{8,10},{9,11},{10,... | collective-permute-start | bytes 786440 | tf_op jit(solution)/shard_map/ppermute | solution.py:299
  38.9 13.1 %collective-permute-start.14 = (bf16[4,128,256]{2,1,0:T(8,128)(2,1)S(1)}, bf16[4,128,256]{2,1,0:T(8,128)(2,1)S(1)}, u32[]{:S(2)}, u32[]{:S(2)}) collective-permute-start(bf16[4,128,256]{2,1,0:T(8,128)(2,1)S(1)} %get-tuple-element.57), channel_id=1, source_target_pairs={{0,3},{1,2},{2,1},{3,0},{4,7},{5,6},{6,5},{7,4},{8,11},{9,10},{10,... | collective-permute-start | bytes 786440 | tf_op jit(solution)/shard_map/ppermute | solution.py:299
  40.4 1.2 %collective-permute-start.8 = (f32[2,4,128]{2,1,0:T(4,128)S(1)}, f32[2,4,128]{2,1,0:T(4,128)S(1)}, u32[]{:S(2)}, u32[]{:S(2)}) collective-permute-start(f32[2,4,128]{2,1,0:T(4,128)S(1)} %get-tuple-element.50), channel_id=1, source_target_pairs={{0,4},{4,0},{8,12},{12,8},{16,20},{20,16},{24,28},{28,24},{1,5},{5... | collective-permute-start | bytes 12296 | tf_op jit(solution)/shard_map/ppermute | solution.py:288
  41.8 3.6 %collective-permute-start.10 = (f32[2,4,128]{2,1,0:T(4,128)S(1)}, f32[2,4,128]{2,1,0:T(4,128)S(1)}, u32[]{:S(2)}, u32[]{:S(2)}) collective-permute-start(f32[2,4,128]{2,1,0:T(4,128)S(1)} %add.9), channel_id=1, source_target_pairs={{0,8},{4,12},{8,0},{12,4},{16,24},{20,28},{24,16},{28,20},{1,9},{5... | collective-permute-start | bytes 12296 | tf_op jit(solution)/shard_map/ppermute | solution.py:288
  45.4 4.5 %collective-permute-start.11 = (f32[2,4,128]{2,1,0:T(4,128)S(1)}, f32[2,4,128]{2,1,0:T(4,128)S(1)}, u32[]{:S(2)}, u32[]{:S(2)}) collective-permute-start(f32[2,4,128]{2,1,0:T(4,128)S(1)} %add.10), channel_id=1, source_target_pairs={{0,16},{4,20},{8,24},{12,28},{16,0},{20,4},{24,8},{28,12},{1,17},{... | collective-permute-start | bytes 12296 | tf_op jit(solution)/shard_map/ppermute | solution.py:288
where the time goes:
time: 53.3 us; the launch traced here: 53 us
  starting transfers between devices  22.8 us (43%)
  Pallas kernels  17.4 us (33%)
  waiting for transfers between devices  11.4 us (21%)
  between operations  0.71 us (1%)
  local copies, waits for them, and re-layouts  0.6 us (1%)
    ppermute x12, starting transfers between devices, exchange_slots(): arrived.append(lax.ppermute(piece, ('dp', 'seq'), pairs))  18.7 us
    pallas_call x2, Pallas kernels, attention(): pl.pallas_call(functools.partial(attention_kernel, shards, first, heads,...  12.6 us
    ppermute x12, waiting for transfers between devices, exchange_slots(): arrived.append(lax.ppermute(piece, ('dp', 'seq'), pairs))  7.38 us
    ppermute x3, starting transfers between devices, exchange(): return lax.ppermute(array, axis, [(i, i ^ k) for i in range(size)])  4.12 us
    ppermute x3, waiting for transfers between devices, exchange(): return lax.ppermute(array, axis, [(i, i ^ k) for i in range(size)])  4.07 us
    pallas_call x2, Pallas kernels, pack(): pl.pallas_call(functools.partial(pack_kernel, shards, local_width, first,...  2.64 us
    pallas_call x2, Pallas kernels, unpack(): pl.pallas_call(functools.partial(unpack_kernel, shards, local_width, firs...  2.17 us
  transfers between devices with their start and end apart: 15, of which 9 were waited for; matrix products, arithmetic and copies ran while one was open for 1% of the time, Pallas kernels for 28%

commit v1 on v0

v1 whole, which is shorter than its diff:
```python
import functools
import math

import jax
import jax.numpy as jnp
from jax import lax
from jax.experimental import pallas as pl
from jax.experimental.pallas import tpu as pltpu
from jax.sharding import PartitionSpec as P

NEGATIVE = -1e30
EPSILON = 1e-06
VMEM_LIMIT = 48 * 1024 * 1024
ANY = pl.BlockSpec(memory_space=pl.ANY)
HBM = pl.BlockSpec(memory_space=pltpu.HBM)
WHOLE = pl.BlockSpec(memory_space=pltpu.VMEM)


def run_copies(copies):
    for copy in copies:
        copy.start()
    for copy in copies:
        copy.wait()


def head_columns(owner, local_width, first, width):
    return pl.ds(pl.multiple_of(owner * local_width + first, 128), width)


def partners(k, shards):
    if shards == 4:
        return ((0, 0), (1, 3), (2, 1), (3, 2))[k]
    bits = shards.bit_length() - 1
    low = (1 << bits // 2) - 1
    return (k, k if bits % 2 else (k & low) << bits // 2 | k >> bits // 2)


def partner_of(k, shards):
    even, odd = partners(k, shards)
    return lax.axis_index("seq") ^ (even + (lax.axis_index("dp") & 1) * (odd - even))


def pack_kernel(items, shards, local_width, width, *refs):
    rows, outs, sems = refs[:4], refs[4:-1], refs[-1]
    run_copies(
        [
            pltpu.make_async_copy(
                rows[a].at[0, :, head_columns(partner_of(k, shards), local_width, first, width)],
                outs[i].at[a],
                sems.at[i, a],
            )
            for i, (k, first) in enumerate(items)
            for a in range(4)
        ]
    )


def pack(items, shards, local_width, width, rows):
    shape = jax.ShapeDtypeStruct((4, rows[0].shape[1], width), rows[0].dtype)
    moved = len(items) * math.prod(shape.shape) * 4
    return pl.pallas_call(
        functools.partial(pack_kernel, items, shards, local_width, width),
        out_shape=[shape] * len(items),
        in_specs=[HBM] * 4,
        out_specs=[ANY] * len(items),
        scratch_shapes=[pltpu.SemaphoreType.DMA((len(items), 4))],
        compiler_params=pltpu.CompilerParams(vmem_limit_bytes=VMEM_LIMIT),
        cost_estimate=pl.CostEstimate(flops=0, bytes_accessed=moved, transcendentals=0),
        name="pack",
    )(*rows)


def unpack_kernel(slots, shards, local_width, first, width, held, *refs):
    pieces, outs, sems = refs[: len(slots)], refs[len(slots) + held : -1], refs[-1]
    run_copies(
        [
            pltpu.make_async_copy(
                piece.at[a],
                outs[a].at[0, :, head_columns(partner_of(k, shards), local_width, first, width)],
                sems.at[k, a],
            )
            for piece, k in zip(pieces, slots)
            for a in range(4)
        ]
    )


def unpack(slots, shards, local_width, first, width, pieces, held):
    tokens = pieces[0].shape[1]
    shape = jax.ShapeDtypeStruct((1, tokens, shards * local_width), pieces[0].dtype)
    moved = sum(piece.size for piece in pieces) * 4
    return pl.pallas_call(
        functools.partial(unpack_kernel, slots, shards, local_width, first, width, len(held)),
        out_shape=[shape] * 4,
        in_specs=[ANY] * (len(slots) + len(held)),
        out_specs=[ANY] * 4,
        input_output_aliases={len(slots) + a: a for a in range(len(held))},
        scratch_shapes=[pltpu.SemaphoreType.DMA((shards, 4))],
        compiler_params=pltpu.CompilerParams(vmem_limit_bytes=VMEM_LIMIT),
        cost_estimate=pl.CostEstimate(flops=0, bytes_accessed=moved, transcendentals=0),
        name="unpack",
    )(*pieces, *held)


def dot_nn(left, right):
    return lax.dot_general(
        left, right, (((1,), (0,)), ((), ())), preferred_element_type=jnp.float32
    )


def dot_nt(left, right):
    return lax.dot_general(
        left, right, (((1,), (1,)), ((), ())), preferred_element_type=jnp.float32
    )


def dot_tn(left, right):
    return lax.dot_general(
        left, right, (((0,), (0,)), ((), ())), preferred_element_type=jnp.float32
    )


def norm_forward(rows, gain, axis):
    inverse = lax.rsqrt(jnp.mean(rows * rows, axis=axis, keepdims=True) + EPSILON)
    unit = rows * inverse
    return (unit * gain).astype(jnp.bfloat16), unit, inverse


def norm_backward(grads, unit, inverse, gain, score_scale, axis):
    scaled = grads * (gain * score_scale)
    along = jnp.mean(scaled * unit, axis=axis, keepdims=True)
    gain_grad = jnp.sum(grads * unit, axis=1 - axis, keepdims=True) * score_scale
    return inverse * (scaled - unit * along), gain_grad


def attend(queries, keys, values, grads, gain_q, gain_k, allowed, block, score_scale):
    tokens = queries.shape[0]
    gain_q = jnp.concatenate([gain_q] * (tokens // gain_q.shape[1]), axis=1)
    turned = queries.T.astype(jnp.float32)
    query_norm, query_unit, query_inverse = norm_forward(turned, gain_q, 0)
    key_norm, key_unit, key_inverse = norm_forward(keys.astype(jnp.float32), gain_k, 1)
    keys_turned, values_turned, grads_turned = key_norm.T, values.T, grads.T
    outs, query_grads = [], []
    key_grad = value_grad = None
    exponent_scale = score_scale * math.log2(math.e)
    for start in range(0, tokens, block):
        span = slice(start, start + block)
        query_block, grads_block = query_norm[:, span], grads_turned[:, span]
        scores = dot_nn(key_norm, query_block)
        if allowed is not None:
            scores = jnp.where(allowed, scores, NEGATIVE)
        row_max = jnp.max(scores, axis=0, keepdims=True)
        shifted = jnp.exp2((scores - row_max) * exponent_scale)
        if allowed is not None:
            shifted = jnp.where(allowed, shifted, 0.0)
        weights = shifted * (1.0 / jnp.sum(shifted, axis=0, keepdims=True))
        weights_low = weights.astype(jnp.bfloat16)
        output = dot_nn(values_turned, weights_low)
        row_delta = jnp.sum(grads_block.astype(jnp.float32) * output, axis=0, keepdims=True)
        grad_probs = dot_nn(values, grads_block)
        grad_scores = (weights * (grad_probs - row_delta)).astype(jnp.bfloat16)
        outs.append(output.astype(jnp.bfloat16))
        query_grads.append(dot_nn(keys_turned, grad_scores))
        value_part = dot_nn(weights_low, grads[span])
        key_part = dot_nt(grad_scores, query_block)
        value_grad = value_part if value_grad is None else value_grad + value_part
        key_grad = key_part if key_grad is None else key_grad + key_part
    join = lambda parts: parts[0] if len(parts) == 1 else jnp.concatenate(parts, axis=1)
    query_grad, gain_grad_q = norm_backward(
        join(query_grads), query_unit, query_inverse, gain_q, score_scale, 0
    )
    key_grad, gain_grad_k = norm_backward(key_grad, key_unit, key_inverse, gain_k, score_scale, 1)
    results = (join(outs).T, query_grad.astype(jnp.bfloat16).T, key_grad, value_grad)
    return results, (gain_grad_q, gain_grad_k)


def attention_kernel(shards, first, heads, has_held, *refs):
    pieces, refs = refs[:shards], refs[shards:]
    (seg_ref, gain_q_ref, gain_k_ref), refs = refs[:3], refs[3:]
    if has_held:
        held_ref, refs = refs[0], refs[1:]
    sent, refs = refs[:shards], refs[shards:]
    gains_ref, inputs, results, in_sems, out_sems = refs
    tokens, head_dim = pieces[0].shape[1], gain_q_ref.shape[1]
    length = shards * tokens
    quarter = length // 4
    score_scale = 1.0 / math.sqrt(head_dim)

    def place(k):
        return pl.ds(pl.multiple_of(partner_of(k, shards) * tokens, tokens), tokens)

    copies = [
        pltpu.make_async_copy(pieces[k].at[a], inputs.at[a, place(k), :], in_sems.at[k, a])
        for k in range(shards)
        for a in range(4)
    ]
    for copy in copies:
        copy.start()

    segments = seg_ref[...].astype(jnp.float32)
    lane = lax.broadcasted_iota(jnp.int32, (1, length), 1)
    middle = jnp.max(jnp.where(lane == length // 2, segments, -1.0), axis=1, keepdims=True)
    before = jnp.sum(jnp.where(segments < middle, 1.0, 0.0), axis=1, keepdims=True)
    row = lax.broadcasted_iota(jnp.int32, (quarter, head_dim), 0).astype(jnp.float32)
    late = row >= before
    late_lanes = lane[:, :quarter].astype(jnp.float32) >= before
    seg_rest = jnp.where(late_lanes, segments[:, 3 * quarter :], segments[:, :quarter])
    seg_lanes = jnp.broadcast_to(seg_rest, (quarter, quarter))
    allowed = seg_lanes == seg_lanes.T

    def turn(row):
        return jnp.broadcast_to(row, (head_dim, head_dim)).T

    for copy in copies:
        copy.wait()

    for head in range(heads):
        columns = slice(head * head_dim, (head + 1) * head_dim)
        image, rest = [], []
        for a in range(4):
            early = inputs[a, :quarter, columns].astype(jnp.float32)
            latest = inputs[a, 3 * quarter :, columns].astype(jnp.float32)
            shared = jnp.where(late, early, latest).astype(jnp.bfloat16)
            image.append(jnp.concatenate([shared, inputs[a, quarter : 3 * quarter, columns]], axis=0))
            rest.append(jnp.where(late, latest, early).astype(jnp.bfloat16))
        own = slice(first + head, first + head + 1)
        gain_q, gain_k = turn(gain_q_ref[own, :]), gain_k_ref[own, :]
        block = min(3 * quarter, 384)
        image_out, image_gains = attend(*image, gain_q, gain_k, None, block, score_scale)
        rest_out, rest_gains = attend(*rest, gain_q, gain_k, allowed, quarter, score_scale)
        for a in range(4):
            shared = image_out[a][:quarter].astype(jnp.float32)
            other = rest_out[a].astype(jnp.float32)
            results[a, :quarter, columns] = jnp.where(late, shared, other).astype(jnp.bfloat16)
            results[a, quarter : 3 * quarter, columns] = image_out[a][quarter:].astype(jnp.bfloat16)
            results[a, 3 * quarter :, columns] = jnp.where(late, other, shared).astype(jnp.bfloat16)
        column = jnp.broadcast_to(image_gains[0] + rest_gains[0], (head_dim, head_dim))
        gains_ref[0, own, :] = column.T[:1]
        gains_ref[1, own, :] = image_gains[1] + rest_gains[1]
    if has_held:
        gains_ref[:, :first, :] = held_ref[:, :first, :]

    run_copies(
        [
            pltpu.make_async_copy(
                results.at[a, place(k), :], sent[k].at[a], out_sems.at[k, a]
            )
            for k in range(shards)
            for a in range(4)
        ]
    )


def attention(shards, first, heads, received, segments, gain_q, gain_k, held):
    tokens, head_dim = received[0].shape[1], gain_q.shape[1]
    width, length = heads * head_dim, shards * tokens
    pieces = [jax.ShapeDtypeStruct((4, tokens, width), jnp.bfloat16)] * shards
    gains = jax.ShapeDtypeStruct((2,) + gain_q.shape, jnp.float32)
    cost = pl.CostEstimate(
        flops=12 * heads * length * length * head_dim,
        bytes_accessed=16 * length * width,
        transcendentals=heads * length * length,
    )
    return pl.pallas_call(
        functools.partial(attention_kernel, shards, first, heads, len(held) > 0),
        out_shape=pieces + [gains],
        in_specs=[ANY] * shards + [WHOLE] * (3 + len(held)),
        out_specs=[ANY] * len(pieces) + [WHOLE],
        scratch_shapes=[
            pltpu.VMEM((4, length, width), jnp.bfloat16),
            pltpu.VMEM((4, length, width), jnp.bfloat16),
            pltpu.SemaphoreType.DMA((shards, 4)),
            pltpu.SemaphoreType.DMA((shards, 4)),
        ],
        compiler_params=pltpu.CompilerParams(vmem_limit_bytes=VMEM_LIMIT),
        cost_estimate=cost,
        name="attention",
    )(*received, segments, gain_q, gain_k, *held)


def exchange(array, axis, size, k):
    return lax.ppermute(array, axis, [(i, i ^ k) for i in range(size)])


def exchange_slots(pieces, packs, shards):
    arrived = []
    for k, piece in enumerate(pieces, start=1):
        pairs = [
            (pack * shards + i, pack * shards + (i ^ partners(k, shards)[pack % 2]))
            for pack in range(packs)
            for i in range(shards)
        ]
        arrived.append(lax.ppermute(piece, ("dp", "seq"), pairs))
    return arrived


def on_device(shards, packs, query_rows, key_rows, value_rows, out_cotangent, segment_ids, gain_query, gain_key):
    rows = tuple(
        pltpu.with_memory_space_constraint(array, pltpu.HBM)
        for array in (query_rows, key_rows, value_rows, out_cotangent)
    )
    local_heads, head_dim = gain_query.shape
    local_width = local_heads * head_dim
    heads = local_heads // 2 if local_heads % 2 == 0 else local_heads
    firsts = range(0, local_heads, heads)
    width = heads * head_dim
    arrived, kept = [], []
    for first in firsts:
        items = [(k, first * head_dim) for k in range(1, shards)]
        if first == firsts[-1]:
            items += [(0, start * head_dim) for start in firsts]
        packed = pack(items, shards, local_width, width, rows)
        arrived.append(exchange_slots(packed[: shards - 1], packs, shards))
        kept += packed[shards - 1 :]
    gains = ()
    returned = []
    for first, own, received in zip(firsts, kept, arrived):
        *pieces, gains = attention(
            shards, first, heads, [own] + received, segment_ids, gain_query, gain_key, gains
        )
        gains = (gains,)
        returned.append(pieces[:1] + exchange_slots(pieces[1:], packs, shards))
    total, step = gains[0], 1
    while step < packs:
        waited = slice(0, -1) if step == 1 else slice(-1, None)
        if step <= 2:
            total, returned[0][waited] = lax.optimization_barrier((total, returned[0][waited]))
        total = total + exchange(total, "dp", packs, step)
        step *= 2
    sums = (total[0], total[1])
    sums, returned[-1][0] = lax.optimization_barrier((sums, returned[-1][0]))
    outs = ()
    for first, pieces in zip(firsts, returned):
        slots = tuple(range(shards))
        parts = [slots[:-1], slots[-1:]] if first == firsts[-1] else [slots]
        for part in parts:
            some = [pieces[k] for k in part]
            outs = unpack(part, shards, local_width, first * head_dim, width, some, outs)
    return (*outs, *sums)


def solution(mesh):
    rows = P("dp", "seq", None)
    gain = P("seq", None)
    return jax.shard_map(
        functools.partial(on_device, mesh.shape["seq"], mesh.shape["dp"]),
        mesh=mesh,
        in_specs=(rows, rows, rows, rows, P("dp", None), gain, gain),
        out_specs=(rows, rows, rows, rows, gain, gain),
        check_vma=False,
    )
```

time: 53.3 us -> 53.1 us (level)
    pallas_call x4 -> x5, Pallas kernels: 4.81 us -> 5.74 us  [the longest x3 2.94 us: unpack(): pl.pallas_call(functools.partial(unpack_kernel, slots, shards, local_widt...]
    ppermute x12, waiting for transfers between devices: 7.38 us -> 6.78 us  [exchange_slots(): arrived.append(lax.ppermute(piece, ('dp', 'seq'), pairs))]
  transfers between devices with their start and end apart: 15 -> 15, of which waited for: 9 -> 9; matrix products, arithmetic and copies ran while one was open for 1% -> 1% of each run, Pallas kernels for 28% -> 30%
where the time goes in v1:
time: 53.1 us; the launch traced here: 52.8 us
  starting transfers between devices  22.4 us (42%)
  Pallas kernels  17.9 us (34%)
  waiting for transfers between devices  11.2 us (21%)
  between operations  0.72 us (1%)
  local copies, waits for them, and re-layouts  0.6 us (1%)
    ppermute x12, starting transfers between devices, exchange_slots(): arrived.append(lax.ppermute(piece, ('dp', 'seq'), pairs))  18.6 us
    pallas_call x2, Pallas kernels, attention(): pl.pallas_call(functools.partial(attention_kernel, shards, first, heads,...  12.2 us
    ppermute x12, waiting for transfers between devices, exchange_slots(): arrived.append(lax.ppermute(piece, ('dp', 'seq'), pairs))  6.78 us
    ppermute x3, waiting for transfers between devices, exchange(): return lax.ppermute(array, axis, [(i, i ^ k) for i in range(size)])  4.39 us
    ppermute x3, starting transfers between devices, exchange(): return lax.ppermute(array, axis, [(i, i ^ k) for i in range(size)])  3.8 us
    pallas_call x3, Pallas kernels, unpack(): pl.pallas_call(functools.partial(unpack_kernel, slots, shards, local_widt...  2.94 us
    pallas_call x2, Pallas kernels, pack(): pl.pallas_call(functools.partial(pack_kernel, items, shards, local_width,...  2.8 us
  transfers between devices with their start and end apart: 15, of which 9 were waited for; matrix products, arithmetic and copies ran while one was open for 1% of the time, Pallas kernels for 30%

profile of v1, /device:TPU:0, one launch (start us, length us, event | category | flops | bytes accessed | tf_op | source)
XLA Modules:
  0.0 52.8 jit_solution(6752622495646617112)
XLA Ops:
  0.6 1.3 %pack.3 = (bf16[4,128,256]{2,1,0:T(8,128)(2,1)S(1)}, bf16[4,128,256]{2,1,0:T(8,128)(2,1)S(1)}, bf16[4,128,256]{2,1,0:T(8,128)(2,1)S(1)}) custom-call(bf16[1,128,2048]{2,1,0:T(8,128)(2,1)} %refs_0_.3, bf16[1,128,2048]{2,1,0:T(8,128)(2,1)} %refs_1_.3, bf16[1,128,2048]{2,1,0:T(8,128)(2,1)} %refs_2_.3, bf16[1,128,2048]{2,1,0:T(8,128)(2,1)} %refs_3_.3), custom_call_target="tpu_custom_call" | custom-call | bytes 1572864 | tf_op jit(solution)/shard_map/pack/pallas_call | solution.py:61
  1.9 3.0 %collective-permute-start.3 = (bf16[4,128,256]{2,1,0:T(8,128)(2,1)S(1)}, bf16[4,128,256]{2,1,0:T(8,128)(2,1)S(1)}, u32[]{:S(2)}, u32[]{:S(2)}) collective-permute-start(bf16[4,128,256]{2,1,0:T(8,128)(2,1)S(1)} %get-tuple-element.50), channel_id=1, source_target_pairs={{0,1},{1,0},{2,3},{3,2},{4,7},{5,6},{6,5},{7,4},{8,9},{9,8},{10,11... | collective-permute-start | bytes 786440 | tf_op jit(solution)/shard_map/ppermute | solution.py:293
  4.9 1.5 %collective-permute-start.4 = (bf16[4,128,256]{2,1,0:T(8,128)(2,1)S(1)}, bf16[4,128,256]{2,1,0:T(8,128)(2,1)S(1)}, u32[]{:S(2)}, u32[]{:S(2)}) collective-permute-start(bf16[4,128,256]{2,1,0:T(8,128)(2,1)S(1)} %get-tuple-element.51), channel_id=1, source_target_pairs={{0,2},{1,3},{2,0},{3,1},{4,5},{5,4},{6,7},{7,6},{8,10},{9,11},{10,... | collective-permute-start | bytes 786440 | tf_op jit(solution)/shard_map/ppermute | solution.py:293
  6.4 0.0 collective-permute-start.5
  6.5 1.5 %pack.2 = (bf16[4,128,256]{2,1,0:T(8,128)(2,1)S(1)}, bf16[4,128,256]{2,1,0:T(8,128)(2,1)S(1)}, bf16[4,128,256]{2,1,0:T(8,128)(2,1)S(1)}, bf16[4,128,256]{2,1,0:T(8,128)(2,1)S(1)}, bf16[4,128,256]{2,1,0:T(8,128)(2,1)S(1)}) custom-call(bf16[1,128,2048]{2,1,0:T(8,128)(2,1)} %refs_0_.3, bf16[1,128,2048]{2,1,0:T(8,128)(2,1)} %refs_1_.3, ...), custom_call_target="tpu_custom_call" | custom-call | bytes 2621440 | tf_op jit(solution)/shard_map/pack/pallas_call | solution.py:61
  8.0 2.0 %collective-permute-start = (bf16[4,128,256]{2,1,0:T(8,128)(2,1)S(1)}, bf16[4,128,256]{2,1,0:T(8,128)(2,1)S(1)}, u32[]{:S(2)}, u32[]{:S(2)}) collective-permute-start(bf16[4,128,256]{2,1,0:T(8,128)(2,1)S(1)} %get-tuple-element.46), channel_id=1, source_target_pairs={{0,1},{1,0},{2,3},{3,2},{4,7},{5,6},{6,5},{7,4},{8,9},{9,8},{10,11... | collective-permute-start | bytes 786440 | tf_op jit(solution)/shard_map/ppermute | solution.py:293
  10.0 1.5 %collective-permute-start.1 = (bf16[4,128,256]{2,1,0:T(8,128)(2,1)S(1)}, bf16[4,128,256]{2,1,0:T(8,128)(2,1)S(1)}, u32[]{:S(2)}, u32[]{:S(2)}) collective-permute-start(bf16[4,128,256]{2,1,0:T(8,128)(2,1)S(1)} %get-tuple-element.47), channel_id=1, source_target_pairs={{0,2},{1,3},{2,0},{3,1},{4,5},{5,4},{6,7},{7,6},{8,10},{9,11},{10,... | collective-permute-start | bytes 786440 | tf_op jit(solution)/shard_map/ppermute | solution.py:293
  11.5 0.3 collective-permute-done.3.refs_1_
  11.8 3.3 %collective-permute-start.2 = (bf16[4,128,256]{2,1,0:T(8,128)(2,1)S(1)}, bf16[4,128,256]{2,1,0:T(8,128)(2,1)S(1)}, u32[]{:S(2)}, u32[]{:S(2)}) collective-permute-start(bf16[4,128,256]{2,1,0:T(8,128)(2,1)S(1)} %get-tuple-element.48), channel_id=1, source_target_pairs={{0,3},{1,2},{2,1},{3,0},{4,6},{5,7},{6,4},{7,5},{8,11},{9,10},{10,... | collective-permute-start | bytes 786440 | tf_op jit(solution)/shard_map/ppermute | solution.py:293
  15.1 4.6 %collective-permute-done.4.refs_2_ = bf16[4,128,256]{2,1,0:T(8,128)(2,1)S(1)} collective-permute-done((bf16[4,128,256]{2,1,0:T(8,128)(2,1)S(1)}, bf16[4,128,256]{2,1,0:T(8,128)(2,1)S(1)}, u32[]{:S(2)}, u32[]{:S(2)}) %collective-permute-start.4) | collective-permute-done | bytes 262176 | tf_op jit(solution)/shard_map/ppermute | solution.py:293
  19.7 0.0 collective-permute-done.5.refs_3_
  19.7 6.1 %attention.2 = (bf16[4,128,256]{2,1,0:T(8,128)(2,1)S(1)}, bf16[4,128,256]{2,1,0:T(8,128)(2,1)S(1)}, bf16[4,128,256]{2,1,0:T(8,128)(2,1)S(1)}, bf16[4,128,256]{2,1,0:T(8,128)(2,1)S(1)}, f32[2,4,128]{2,1,0:T(4,128)S(1)}) custom-call(bf16[4,128,256]{2,1,0:T(8,128)(2,1)S(1)} %get-tuple-element.49.refs_0_, ...), custom_call_target="tpu_custom_call" | custom-call | flops 805306368 | bytes 2097152 | tf_op jit(solution)/shard_map/attention/pallas_call | solution.py:264
  25.8 1.2 %collective-permute-start.7 = (bf16[4,128,256]{2,1,0:T(8,128)(2,1)S(1)}, bf16[4,128,256]{2,1,0:T(8,128)(2,1)S(1)}, u32[]{:S(2)}, u32[]{:S(2)}) collective-permute-start(bf16[4,128,256]{2,1,0:T(8,128)(2,1)S(1)} %get-tuple-element.57), channel_id=1, source_target_pairs={{0,1},{1,0},{2,3},{3,2},{4,7},{5,6},{6,5},{7,4},{8,9},{9,8},{10,11... | collective-permute-start | bytes 786440 | tf_op jit(solution)/shard_map/ppermute | solution.py:293
  27.0 1.0 %collective-permute-start.8 = (bf16[4,128,256]{2,1,0:T(8,128)(2,1)S(1)}, bf16[4,128,256]{2,1,0:T(8,128)(2,1)S(1)}, u32[]{:S(2)}, u32[]{:S(2)}) collective-permute-start(bf16[4,128,256]{2,1,0:T(8,128)(2,1)S(1)} %get-tuple-element.58), channel_id=1, source_target_pairs={{0,2},{1,3},{2,0},{3,1},{4,5},{5,4},{6,7},{7,6},{8,10},{9,11},{10,... | collective-permute-start | bytes 786440 | tf_op jit(solution)/shard_map/ppermute | solution.py:293
  27.9 1.4 %collective-permute-start.10 = (bf16[4,128,256]{2,1,0:T(8,128)(2,1)S(1)}, bf16[4,128,256]{2,1,0:T(8,128)(2,1)S(1)}, u32[]{:S(2)}, u32[]{:S(2)}) collective-permute-start(bf16[4,128,256]{2,1,0:T(8,128)(2,1)S(1)} %get-tuple-element.60), channel_id=1, source_target_pairs={{0,3},{1,2},{2,1},{3,0},{4,6},{5,7},{6,4},{7,5},{8,11},{9,10},{10,... | collective-permute-start | bytes 786440 | tf_op jit(solution)/shard_map/ppermute | solution.py:293
  29.3 0.4 collective-permute-done.1.refs_2_
  29.7 0.8 %collective-permute-done.2.refs_3_ = bf16[4,128,256]{2,1,0:T(8,128)(2,1)S(1)} collective-permute-done((bf16[4,128,256]{2,1,0:T(8,128)(2,1)S(1)}, bf16[4,128,256]{2,1,0:T(8,128)(2,1)S(1)}, u32[]{:S(2)}, u32[]{:S(2)}) %collective-permute-start.2) | collective-permute-done | bytes 262176 | tf_op jit(solution)/shard_map/ppermute | solution.py:293
  30.5 6.1 %attention.3 = (bf16[4,128,256]{2,1,0:T(8,128)(2,1)S(1)}, bf16[4,128,256]{2,1,0:T(8,128)(2,1)S(1)}, bf16[4,128,256]{2,1,0:T(8,128)(2,1)S(1)}, bf16[4,128,256]{2,1,0:T(8,128)(2,1)S(1)}, f32[2,4,128]{2,1,0:T(4,128)S(1)}) custom-call(bf16[4,128,256]{2,1,0:T(8,128)(2,1)S(1)} %get-tuple-element.45.refs_0_, bf16[4,128,256]{2,1,0:T(8,128)(2,1)S(1)} %collective-permute-done.refs_1_, ...), custom_call_target="tpu_custom_call" | custom-call | flops 805306368 | bytes 2097152 | tf_op jit(solution)/shard_map/attention/pallas_call | solution.py:264
  36.6 0.3 collective-permute-start.13
  36.9 2.0 %collective-permute-start.14 = (bf16[4,128,256]{2,1,0:T(8,128)(2,1)S(1)}, bf16[4,128,256]{2,1,0:T(8,128)(2,1)S(1)}, u32[]{:S(2)}, u32[]{:S(2)}) collective-permute-start(bf16[4,128,256]{2,1,0:T(8,128)(2,1)S(1)} %get-tuple-element.65), channel_id=1, source_target_pairs={{0,2},{1,3},{2,0},{3,1},{4,5},{5,4},{6,7},{7,6},{8,10},{9,11},{10,... | collective-permute-start | bytes 786440 | tf_op jit(solution)/shard_map/ppermute | solution.py:293
  38.9 1.4 %collective-permute-start.6 = (bf16[4,128,256]{2,1,0:T(8,128)(2,1)S(1)}, bf16[4,128,256]{2,1,0:T(8,128)(2,1)S(1)}, u32[]{:S(2)}, u32[]{:S(2)}) collective-permute-start(bf16[4,128,256]{2,1,0:T(8,128)(2,1)S(1)} %get-tuple-element.54), channel_id=1, source_target_pairs={{0,3},{1,2},{2,1},{3,0},{4,6},{5,7},{6,4},{7,5},{8,11},{9,10},{10,... | collective-permute-start | bytes 786440 | tf_op jit(solution)/shard_map/ppermute | solution.py:293
  40.3 0.6 %collective-permute-done.8.refs_2_ = bf16[4,128,256]{2,1,0:T(8,128)(2,1)S(1)} collective-permute-done((bf16[4,128,256]{2,1,0:T(8,128)(2,1)S(1)}, bf16[4,128,256]{2,1,0:T(8,128)(2,1)S(1)}, u32[]{:S(2)}, u32[]{:S(2)}) %collective-permute-start.8) | collective-permute-done | bytes 262176 | tf_op jit(solution)/shard_map/ppermute | solution.py:293
  40.9 1.2 %collective-permute-done.9 = f32[2,4,128]{2,1,0:T(4,128)S(1)} collective-permute-done((f32[2,4,128]{2,1,0:T(4,128)S(1)}, f32[2,4,128]{2,1,0:T(4,128)S(1)}, u32[]{:S(2)}, u32[]{:S(2)}) %collective-permute-start.9) | collective-permute-done | bytes 4128 | tf_op jit(solution)/shard_map/ppermute | solution.py:282
  42.1 1.4 %collective-permute-start.11 = (f32[2,4,128]{2,1,0:T(4,128)S(1)}, f32[2,4,128]{2,1,0:T(4,128)S(1)}, u32[]{:S(2)}, u32[]{:S(2)}) collective-permute-start(f32[2,4,128]{2,1,0:T(4,128)S(1)} %add.9), channel_id=1, source_target_pairs={{0,8},{4,12},{8,0},{12,4},{16,24},{20,28},{24,16},{28,20},{1,9},{5... | collective-permute-start | bytes 12296 | tf_op jit(solution)/shard_map/ppermute | solution.py:282
  43.4 2.2 %collective-permute-done.11 = f32[2,4,128]{2,1,0:T(4,128)S(1)} collective-permute-done((f32[2,4,128]{2,1,0:T(4,128)S(1)}, f32[2,4,128]{2,1,0:T(4,128)S(1)}, u32[]{:S(2)}, u32[]{:S(2)}) %collective-permute-start.11) | collective-permute-done | bytes 4128 | tf_op jit(solution)/shard_map/ppermute | solution.py:282
  45.7 2.4 %collective-permute-start.12 = (f32[2,4,128]{2,1,0:T(4,128)S(1)}, f32[2,4,128]{2,1,0:T(4,128)S(1)}, u32[]{:S(2)}, u32[]{:S(2)}) collective-permute-start(f32[2,4,128]{2,1,0:T(4,128)S(1)} %add.10), channel_id=1, source_target_pairs={{0,16},{4,20},{8,24},{12,28},{16,0},{20,4},{24,8},{28,12},{1,17},{... | collective-permute-start | bytes 12296 | tf_op jit(solution)/shard_map/ppermute | solution.py:282
  48.1 1.1 %unpack.3 = (bf16[1,128,2048]{2,1,0:T(8,128)(2,1)}, bf16[1,128,2048]{2,1,0:T(8,128)(2,1)}, bf16[1,128,2048]{2,1,0:T(8,128)(2,1)}, bf16[1,128,2048]{2,1,0:T(8,128)(2,1)}) custom-call(bf16[4,128,256]{2,1,0:T(8,128)(2,1)S(1)} %get-tuple-element.66.refs_0_, bf16[4,128,256]{2,1,0:T(8,128)(2,1)S(1)} %collective-permute-done.7.refs_1_, ...), custom_call_target="tpu_custom_call" | custom-call | bytes 2097152 | tf_op jit(solution)/shard_map/unpack/pallas_call | solution.py:92
  49.2 1.0 %collective-permute-done.12 = f32[2,4,128]{2,1,0:T(4,128)S(1)} collective-permute-done((f32[2,4,128]{2,1,0:T(4,128)S(1)}, f32[2,4,128]{2,1,0:T(4,128)S(1)}, u32[]{:S(2)}, u32[]{:S(2)}) %collective-permute-start.12) | collective-permute-done | bytes 4128 | tf_op jit(solution)/shard_map/ppermute | solution.py:282
  50.2 0.6 %slice_bitcast_fusion = (f32[4,128]{1,0:T(4,128)}, f32[4,128]{1,0:T(4,128)}) fusion(f32[2,4,128]{2,1,0:T(4,128)S(1)} %add.11), kind=kLoop, calls=%fused_computation | loop fusion | bytes 8192 | tf_op jit(solution)/shard_map/squeeze | solution.py:330
  50.8 0.2 collective-permute-done.14.refs_2_
  50.9 1.0 %unpack.4 = (bf16[1,128,2048]{2,1,0:T(8,128)(2,1)}, bf16[1,128,2048]{2,1,0:T(8,128)(2,1)}, bf16[1,128,2048]{2,1,0:T(8,128)(2,1)}, bf16[1,128,2048]{2,1,0:T(8,128)(2,1)}) custom-call(bf16[4,128,256]{2,1,0:T(8,128)(2,1)S(1)} %get-tuple-element.63.refs_0_, ...), custom_call_target="tpu_custom_call", output_to_operand_aliasing={{0}: (3, {}), {1}: (4, {}), {2}: (5, {}), {3}: (6, {})} | custom-call | bytes 1572864 | tf_op jit(solution)/shard_map/unpack/pallas_call | solution.py:92
  51.9 0.9 %unpack.5 = (bf16[1,128,2048]{2,1,0:T(8,128)(2,1)}, bf16[1,128,2048]{2,1,0:T(8,128)(2,1)}, bf16[1,128,2048]{2,1,0:T(8,128)(2,1)}, bf16[1,128,2048]{2,1,0:T(8,128)(2,1)}) custom-call(bf16[4,128,256]{2,1,0:T(8,128)(2,1)S(1)} %collective-permute-done.6.refs_0_, ...), custom_call_target="tpu_custom_call", output_to_operand_aliasing={{0}: (1, {}), {1}: (2, {}), {2}: (3, {}), {3}: (4, {})} | custom-call | bytes 524288 | tf_op jit(solution)/shard_map/unpack/pallas_call | solution.py:92
  (15 shorter events, 0.0 us)
Async XLA Ops:
  1.9 9.9 %collective-permute-start.3 = (bf16[4,128,256]{2,1,0:T(8,128)(2,1)S(1)}, bf16[4,128,256]{2,1,0:T(8,128)(2,1)S(1)}, u32[]{:S(2)}, u32[]{:S(2)}) collective-permute-start(bf16[4,128,256]{2,1,0:T(8,128)(2,1)S(1)} %get-tuple-element.50), channel_id=1, source_target_pairs={{0,1},{1,0},{2,3},{3,2},{4,7},{5,6},{6,5},{7,4},{8,9},{9,8},{10,11... | collective-permute-start | bytes 786440 | tf_op jit(solution)/shard_map/ppermute | solution.py:293
  4.9 14.7 %collective-permute-start.4 = (bf16[4,128,256]{2,1,0:T(8,128)(2,1)S(1)}, bf16[4,128,256]{2,1,0:T(8,128)(2,1)S(1)}, u32[]{:S(2)}, u32[]{:S(2)}) collective-permute-start(bf16[4,128,256]{2,1,0:T(8,128)(2,1)S(1)} %get-tuple-element.51), channel_id=1, source_target_pairs={{0,2},{1,3},{2,0},{3,1},{4,5},{5,4},{6,7},{7,6},{8,10},{9,11},{10,... | collective-permute-start | bytes 786440 | tf_op jit(solution)/shard_map/ppermute | solution.py:293
  6.4 13.2 %collective-permute-start.5 = (bf16[4,128,256]{2,1,0:T(8,128)(2,1)S(1)}, bf16[4,128,256]{2,1,0:T(8,128)(2,1)S(1)}, u32[]{:S(2)}, u32[]{:S(2)}) collective-permute-start(bf16[4,128,256]{2,1,0:T(8,128)(2,1)S(1)} %get-tuple-element.52), channel_id=1, source_target_pairs={{0,3},{1,2},{2,1},{3,0},{4,6},{5,7},{6,4},{7,5},{8,11},{9,10},{10,... | collective-permute-start | bytes 786440 | tf_op jit(solution)/shard_map/ppermute | solution.py:293
  6.5 13.2 %copy-start.2 = (f32[4,128]{1,0:T(4,128)S(1)}, f32[4,128]{1,0:T(4,128)}, u32[]{:S(2)}) copy-start(f32[4,128]{1,0:T(4,128)} %refs_6_.3) | copy-start | bytes 6148
  8.0 19.9 %collective-permute-start = (bf16[4,128,256]{2,1,0:T(8,128)(2,1)S(1)}, bf16[4,128,256]{2,1,0:T(8,128)(2,1)S(1)}, u32[]{:S(2)}, u32[]{:S(2)}) collective-permute-start(bf16[4,128,256]{2,1,0:T(8,128)(2,1)S(1)} %get-tuple-element.46), channel_id=1, source_target_pairs={{0,1},{1,0},{2,3},{3,2},{4,7},{5,6},{6,5},{7,4},{8,9},{9,8},{10,11... | collective-permute-start | bytes 786440 | tf_op jit(solution)/shard_map/ppermute | solution.py:293
  10.0 9.7 %copy-start.1 = (f32[4,128]{1,0:T(4,128)S(1)}, f32[4,128]{1,0:T(4,128)}, u32[]{:S(2)}) copy-start(f32[4,128]{1,0:T(4,128)} %refs_5_.3) | copy-start | bytes 6148
  10.0 9.7 %copy-start = (s32[1,512]{1,0:T(1,128)S(1)}, s32[1,512]{1,0:T(1,128)}, u32[]{:S(2)}) copy-start(s32[1,512]{1,0:T(1,128)} %refs_4_.3) | copy-start | bytes 6148
  10.0 19.7 %collective-permute-start.1 = (bf16[4,128,256]{2,1,0:T(8,128)(2,1)S(1)}, bf16[4,128,256]{2,1,0:T(8,128)(2,1)S(1)}, u32[]{:S(2)}, u32[]{:S(2)}) collective-permute-start(bf16[4,128,256]{2,1,0:T(8,128)(2,1)S(1)} %get-tuple-element.47), channel_id=1, source_target_pairs={{0,2},{1,3},{2,0},{3,1},{4,5},{5,4},{6,7},{7,6},{8,10},{9,11},{10,... | collective-permute-start | bytes 786440 | tf_op jit(solution)/shard_map/ppermute | solution.py:293
  11.8 18.7 %collective-permute-start.2 = (bf16[4,128,256]{2,1,0:T(8,128)(2,1)S(1)}, bf16[4,128,256]{2,1,0:T(8,128)(2,1)S(1)}, u32[]{:S(2)}, u32[]{:S(2)}) collective-permute-start(bf16[4,128,256]{2,1,0:T(8,128)(2,1)S(1)} %get-tuple-element.48), channel_id=1, source_target_pairs={{0,3},{1,2},{2,1},{3,0},{4,6},{5,7},{6,4},{7,5},{8,11},{9,10},{10,... | collective-permute-start | bytes 786440 | tf_op jit(solution)/shard_map/ppermute | solution.py:293
  25.8 13.2 %collective-permute-start.7 = (bf16[4,128,256]{2,1,0:T(8,128)(2,1)S(1)}, bf16[4,128,256]{2,1,0:T(8,128)(2,1)S(1)}, u32[]{:S(2)}, u32[]{:S(2)}) collective-permute-start(bf16[4,128,256]{2,1,0:T(8,128)(2,1)S(1)} %get-tuple-element.57), channel_id=1, source_target_pairs={{0,1},{1,0},{2,3},{3,2},{4,7},{5,6},{6,5},{7,4},{8,9},{9,8},{10,11... | collective-permute-start | bytes 786440 | tf_op jit(solution)/shard_map/ppermute | solution.py:293
  27.0 13.9 %collective-permute-start.8 = (bf16[4,128,256]{2,1,0:T(8,128)(2,1)S(1)}, bf16[4,128,256]{2,1,0:T(8,128)(2,1)S(1)}, u32[]{:S(2)}, u32[]{:S(2)}) collective-permute-start(bf16[4,128,256]{2,1,0:T(8,128)(2,1)S(1)} %get-tuple-element.58), channel_id=1, source_target_pairs={{0,2},{1,3},{2,0},{3,1},{4,5},{5,4},{6,7},{7,6},{8,10},{9,11},{10,... | collective-permute-start | bytes 786440 | tf_op jit(solution)/shard_map/ppermute | solution.py:293
  27.9 14.1 %collective-permute-start.10 = (bf16[4,128,256]{2,1,0:T(8,128)(2,1)S(1)}, bf16[4,128,256]{2,1,0:T(8,128)(2,1)S(1)}, u32[]{:S(2)}, u32[]{:S(2)}) collective-permute-start(bf16[4,128,256]{2,1,0:T(8,128)(2,1)S(1)} %get-tuple-element.60), channel_id=1, source_target_pairs={{0,3},{1,2},{2,1},{3,0},{4,6},{5,7},{6,4},{7,5},{8,11},{9,10},{10,... | collective-permute-start | bytes 786440 | tf_op jit(solution)/shard_map/ppermute | solution.py:293
  36.6 14.2 %collective-permute-start.13 = (bf16[4,128,256]{2,1,0:T(8,128)(2,1)S(1)}, bf16[4,128,256]{2,1,0:T(8,128)(2,1)S(1)}, u32[]{:S(2)}, u32[]{:S(2)}) collective-permute-start(bf16[4,128,256]{2,1,0:T(8,128)(2,1)S(1)} %get-tuple-element.64), channel_id=1, source_target_pairs={{0,1},{1,0},{2,3},{3,2},{4,7},{5,6},{6,5},{7,4},{8,9},{9,8},{10,11... | collective-permute-start | bytes 786440 | tf_op jit(solution)/shard_map/ppermute | solution.py:293
  36.9 14.0 %collective-permute-start.14 = (bf16[4,128,256]{2,1,0:T(8,128)(2,1)S(1)}, bf16[4,128,256]{2,1,0:T(8,128)(2,1)S(1)}, u32[]{:S(2)}, u32[]{:S(2)}) collective-permute-start(bf16[4,128,256]{2,1,0:T(8,128)(2,1)S(1)} %get-tuple-element.65), channel_id=1, source_target_pairs={{0,2},{1,3},{2,0},{3,1},{4,5},{5,4},{6,7},{7,6},{8,10},{9,11},{10,... | collective-permute-start | bytes 786440 | tf_op jit(solution)/shard_map/ppermute | solution.py:293
  38.9 13.0 %collective-permute-start.6 = (bf16[4,128,256]{2,1,0:T(8,128)(2,1)S(1)}, bf16[4,128,256]{2,1,0:T(8,128)(2,1)S(1)}, u32[]{:S(2)}, u32[]{:S(2)}) collective-permute-start(bf16[4,128,256]{2,1,0:T(8,128)(2,1)S(1)} %get-tuple-element.54), channel_id=1, source_target_pairs={{0,3},{1,2},{2,1},{3,0},{4,6},{5,7},{6,4},{7,5},{8,11},{9,10},{10,... | collective-permute-start | bytes 786440 | tf_op jit(solution)/shard_map/ppermute | solution.py:293
  40.9 1.2 %collective-permute-start.9 = (f32[2,4,128]{2,1,0:T(4,128)S(1)}, f32[2,4,128]{2,1,0:T(4,128)S(1)}, u32[]{:S(2)}, u32[]{:S(2)}) collective-permute-start(f32[2,4,128]{2,1,0:T(4,128)S(1)} %get-tuple-element.59), channel_id=1, source_target_pairs={{0,4},{4,0},{8,12},{12,8},{16,20},{20,16},{24,28},{28,24},{1,5},{5... | collective-permute-start | bytes 12296 | tf_op jit(solution)/shard_map/ppermute | solution.py:282
  42.1 3.6 %collective-permute-start.11 = (f32[2,4,128]{2,1,0:T(4,128)S(1)}, f32[2,4,128]{2,1,0:T(4,128)S(1)}, u32[]{:S(2)}, u32[]{:S(2)}) collective-permute-start(f32[2,4,128]{2,1,0:T(4,128)S(1)} %add.9), channel_id=1, source_target_pairs={{0,8},{4,12},{8,0},{12,4},{16,24},{20,28},{24,16},{28,20},{1,9},{5... | collective-permute-start | bytes 12296 | tf_op jit(solution)/shard_map/ppermute | solution.py:282
  45.7 4.5 %collective-permute-start.12 = (f32[2,4,128]{2,1,0:T(4,128)S(1)}, f32[2,4,128]{2,1,0:T(4,128)S(1)}, u32[]{:S(2)}, u32[]{:S(2)}) collective-permute-start(f32[2,4,128]{2,1,0:T(4,128)S(1)} %add.10), channel_id=1, source_target_pairs={{0,16},{4,20},{8,24},{12,28},{16,0},{20,4},{24,8},{28,12},{1,17},{... | collective-permute-start | bytes 12296 | tf_op jit(solution)/shard_map/ppermute | solution.py:282
